TPU v7x, 128 devices: a whole 4x4x4 slice. The times are simulated.
128 devices in a mesh: layer: 4 (over x_lo, core), tile: 32 (over z, x_hi, y).
Axes of the slice: x: 4 (x_hi: 2, x_lo: 2; x = x_hi * 2 + x_lo), y: 4, z: 4, core: 2. Of those that a mesh axis runs over, the one named last changes fastest.
Arguments:
- load_current: float32 [8, 4096, 2816], P('layer', 'tile'), may hold values from 0.05 to 1
- metal_class: int32 [8, 4096, 2816], P('layer', 'tile'), may hold values from 0 to 15
- via_mask: int32 [8, 4096, 2816], P('layer', 'tile'), may hold values 0 or 1
- temp_prior: float32 [8, 4096, 2816], P('layer', 'tile'), may hold values from 25 to 125
- drop_prior: float32 [8, 4096, 2816], P('layer', 'tile'), may hold values from 0 to 1
- class_conductance: float32 [8, 16], P('layer'), may hold values from 0.5 to 8
Outputs:
- drop_next: float32 [8, 4096, 2816], P('layer', 'tile')
- temp_rise: float32 [8, 4096, 2816], P('layer', 'tile')
Inputs may be any that keep to these rules, and one draw needn't show every extreme that they name: `metal_class`: class indices.
All inputs are finite; a program needn't handle non-finite values. No bound on the sum of `via_mask` on one device may be relied on, other than what follows from the above.
Results may differ from a plain program's by a relative error of at most 0.0003.
Values sent between devices are 32-bit elements; how exact they have to be, the bound alone decides.
A program may use at most 192 MiB of HBM per device.

v0:
```python
import jax
import jax.numpy as jnp
from jax import lax
from jax.sharding import PartitionSpec as P

centre = 1.0
half_width = 0.9


def with_halo(block, sides, width):
    for axis, dim in sides:
        count = lax.axis_size(axis)
        forward = [(i, i + 1) for i in range(count - 1)]
        backward = [(target, source) for source, target in forward]
        low = lax.ppermute(
            lax.slice_in_dim(block, block.shape[dim] - width, None, axis=dim), axis, forward
        )
        high = lax.ppermute(lax.slice_in_dim(block, 0, width, axis=dim), axis, backward)
        block = jnp.concatenate([low, block, high], axis=dim)
    return block


def harmonic(first, second):
    total = first + second
    safe = jnp.where(total > 0, total, 1.0)
    return jnp.where(total > 0, 2.0 * first * second / safe, 0.0)


def node_conductance(metal_class, table, temp_prior):
    base = jnp.zeros(metal_class.shape, jnp.float32)
    for member in range(table.shape[1]):
        base = base + jnp.where(metal_class == member, table[:, member][:, None, None], 0.0)
    return base / (1.0 + 0.0039 * (temp_prior - 25.0))


def direction_factors(strata):
    along_rows = jnp.where(strata % 2 == 0, 1.0, 0.25).astype(jnp.float32)[:, None, None]
    return (along_rows, 1.25 - along_rows)


def pad_cols(field):
    return jnp.pad(field, ((0, 0), (0, 0), (1, 1)))


def edge_set(padded_g, along_rows, along_cols, shunt):
    own = padded_g[:, 1:-1]
    north = harmonic(own, padded_g[:, :-2]) * along_rows
    south = harmonic(own, padded_g[:, 2:]) * along_rows
    side = pad_cols(own)
    west = harmonic(own, side[..., :-2]) * along_cols
    east = harmonic(own, side[..., 2:]) * along_cols
    total = north + south + west + east + shunt
    return (north, south, west, east, total)


def scaled_residual(padded_x, load, edges, safe_total):
    north, south, west, east, total = edges
    own = padded_x[:, 1:-1]
    side = pad_cols(own)
    image = (
        total * own
        - north * padded_x[:, :-2]
        - south * padded_x[:, 2:]
        - west * side[..., :-2]
        - east * side[..., 2:]
    )
    return (load - image) / safe_total


def joule(padded_x, edges, shunt):
    north, south, west, east, total = edges
    own = padded_x[:, 1:-1]
    side = pad_cols(own)
    heat = north * (own - padded_x[:, :-2]) ** 2 + south * (own - padded_x[:, 2:]) ** 2
    heat = heat + west * (own - side[..., :-2]) ** 2 + east * (own - side[..., 2:]) ** 2
    return 0.1 * (0.5 * heat + shunt * own * own)


def column_solve(heat, vertical_flux):
    node_count = heat.shape[0]
    ratio_values = []
    eliminated_factors = []
    for layer_level in range(node_count):
        pivot_value = 0.2 + vertical_flux[layer_level]
        numerator = heat[layer_level]
        if layer_level > 0:
            pivot_value = (
                pivot_value
                + vertical_flux[layer_level - 1]
                - vertical_flux[layer_level - 1] * ratio_values[-1]
            )
            numerator = numerator + vertical_flux[layer_level - 1] * eliminated_factors[-1]
        ratio_values.append(vertical_flux[layer_level] / pivot_value)
        eliminated_factors.append(numerator / pivot_value)
    result_values = [None] * node_count
    result_values[node_count - 1] = eliminated_factors[node_count - 1]
    for layer_level in range(node_count - 2, -1, -1):
        result_values[layer_level] = (
            eliminated_factors[layer_level]
            + ratio_values[layer_level] * result_values[layer_level + 1]
        )
    return jnp.stack(result_values)


def chebyshev_tail(step_one, drop_one, second):
    rho_one = half_width / centre
    rho_two = 1.0 / (2.0 * centre / half_width - rho_one)
    step_two = rho_two * rho_one * step_one + 2.0 * rho_two / half_width * second
    return drop_one + step_two


def local(load_current, metal_class, via_mask, temp_prior, drop_prior, class_conductance):
    layers_here = load_current.shape[0]
    strata = lax.axis_index("layer") * layers_here + jnp.arange(layers_here, dtype=jnp.int32)
    cond = node_conductance(metal_class, class_conductance, temp_prior)
    along_rows, along_cols = direction_factors(strata)
    vias = via_mask.astype(jnp.float32)
    shunt = cond * (0.05 + 0.5 * vias)
    stacked = jnp.stack([cond, drop_prior])
    widened = with_halo(stacked, (("tile", 2),), 1)
    edges = edge_set(widened[0], along_rows, along_cols, shunt)
    first = scaled_residual(widened[1], load_current, edges, edges[4])
    step_one = first / centre
    drop_one = drop_prior + step_one
    padded_one = with_halo(drop_one, (("tile", 1),), 1)
    second = scaled_residual(padded_one, load_current, edges, edges[4])
    drop_next = chebyshev_tail(step_one, drop_one, second)
    padded_next = with_halo(drop_next, (("tile", 1),), 1)
    heat = joule(padded_next, edges, shunt)
    vertical_flux = (1.0 + 4.0 * vias) / (1.0 + 0.002 * (temp_prior - 25.0))
    solved = column_solve(
        lax.all_to_all(heat, "layer", split_axis=1, concat_axis=0, tiled=True),
        lax.all_to_all(vertical_flux, "layer", split_axis=1, concat_axis=0, tiled=True),
    )
    temp_rise = lax.all_to_all(solved, "layer", split_axis=0, concat_axis=1, tiled=True)
    return (drop_next, temp_rise)


def solution(mesh):
    in_specs = (
        P("layer", "tile", None),
        P("layer", "tile", None),
        P("layer", "tile", None),
        P("layer", "tile", None),
        P("layer", "tile", None),
        P("layer", None),
    )
    out_specs = (P("layer", "tile", None), P("layer", "tile", None))
    return jax.shard_map(local, mesh=mesh, in_specs=in_specs, out_specs=out_specs, check_vma=False)
```

profile of v0, /device:TPU:99, one launch (start us, length us, event | category | flops | bytes accessed | tf_op | source)
XLA Modules:
  0.0 230.0 jit_solution(2508119317438929149)
XLA Ops:
  0.6 1.7 slice_reduce_fusion.15
  2.3 0.0 copy-start.6
  2.4 6.7 %add_divide_fusion.1 = f32[2,128,2816]{2,1,0:T(8,128)S(1)} fusion(s32[2,128,2816]{2,1,0:T(8,128)} %param.7, f32[2,128,2816]{2,1,0:T(8,128)} %param.9, f32[2]{0:T(128)S(1)} %get-tuple-element.18, f32[2]{0:T(128)S(1)} %get-tuple-element.19, f32[2]{0:T(128)S(1)} %get-tuple-element.5, f32[2]{0:T(128)S(1)} %get-tuple-element.6, f32[2]{0:T(128)S(1)} %get-tuple-element.7, ...), kind=kLoop, calls=%fused_computation.76 | loop fusion | flops 36765696 | bytes 8650880 | tf_op jit(solution)/shard_map/div | solution.py:33
  9.0 0.0 copy-done.6
  9.1 0.1 pad_maximum_fusion.6
  9.1 3.2 %collective-permute-start = (f32[2,2,1,2816]{3,2,1,0:T(1,128)S(1)}, f32[2,2,1,2816]{3,2,1,0:T(1,128)S(1)}, u32[]{:S(2)}, u32[]{:S(2)}) collective-permute-start(f32[2,2,1,2816]{3,2,1,0:T(1,128)S(1)} %get-tuple-element.43), channel_id=1, source_target_pairs={{0,1},{1,2},{2,3},{3,4},{4,5},{5,6},{6,7},{7,8},{8,9},{9,10},{10,1... | collective-permute-start | bytes 135176 | tf_op jit(solution)/shard_map/ppermute | solution.py:15
  12.3 6.6 %collective-permute-start.1 = (f32[2,2,1,2816]{3,2,1,0:T(1,128)S(1)}, f32[2,2,1,2816]{3,2,1,0:T(1,128)S(1)}, u32[]{:S(2)}, u32[]{:S(2)}) collective-permute-start(f32[2,2,1,2816]{3,2,1,0:T(1,128)S(1)} %get-tuple-element.44), channel_id=1, source_target_pairs={{1,0},{2,1},{3,2},{4,3},{5,4},{6,5},{7,6},{8,7},{9,8},{10,9},{11,1... | collective-permute-start | bytes 135176 | tf_op jit(solution)/shard_map/ppermute | solution.py:18
  19.0 0.0 collective-permute-done
  19.0 1.1 collective-permute-done.1
  20.1 2.2 pad_maximum_fusion
  22.3 0.5 slice_bitcast_fusion.1
  22.8 0.0 copy-start
  22.8 0.0 copy-start.1
  22.8 1.9 slice.265
  24.7 0.6 copy-done
  25.3 0.9 copy-done.1
  26.2 1.8 slice.269
  28.0 23.3 %fusion.62 = (f32[2,128,2816]{2,1,0:T(8,128)}, f32[2,128,2816]{2,1,0:T(8,128)}, f32[2,128,2816]{2,1,0:T(8,128)}, f32[2,128,2816]{2,1,0:T(8,128)}, f32[2,128,2816]{2,1,0:T(8,128)}, /*index=5*/f32[2,128,2816]{2,1,0:T(8,128)}) fusion(f32[2,128,2816]{2,1,0:T(8,128)} %param.10, f32[2,128,2816]{2,1,0:T(8,128)} %param.6, f32[2,128,2816]{2,1,0:T(8,128)} %slice.269, ...), kind=kLoop, calls=%fused_computation.146 | loop fusion | flops 36044800 | bytes 49020944 | tf_op jit(solution)/shard_map/add | solution.py:124
  51.3 1.0 fusion.69
  52.3 1.9 collective-permute-start.2
  54.2 8.2 %collective-permute-start.3 = (f32[2,1,2816]{2,1,0:T(1,128)S(1)}, f32[2,1,2816]{2,1,0:T(1,128)S(1)}, u32[]{:S(2)}, u32[]{:S(2)}) collective-permute-start(f32[2,1,2816]{2,1,0:T(1,128)S(1)} %get-tuple-element.50), channel_id=1, source_target_pairs={{1,0},{2,1},{3,2},{4,3},{5,4},{6,5},{7,6},{8,7},{9,8},{10,9},{11,1... | collective-permute-start | bytes 67592 | tf_op jit(solution)/shard_map/ppermute | solution.py:18
  62.4 0.0 collective-permute-done.2
  62.4 0.9 collective-permute-done.3
  63.3 0.0 copy-start.2
  63.3 0.0 copy-start.3
  63.3 0.0 copy-start.4
  63.3 0.0 copy-start.5
  63.3 15.0 %fusion.13 = f32[2,128,2816]{2,1,0:T(8,128)} fusion(f32[2,128,2816]{2,1,0:T(8,128)} %get-tuple-element.35, f32[2,128,2816]{2,1,0:T(8,128)} %param.6, f32[2,128,2816]{2,1,0:T(8,128)} %get-tuple-element.40, f32[2,128,2816]{2,1,0:T(8,128)} %get-tuple-element.39, f32[2,128,2816]{2,1,0:T(8,128)} %get-tuple-element.38, ...), kind=kLoop, calls=%fused_computation.33 | loop fusion | flops 18022400 | bytes 28880896 | tf_op jit(solution)/shard_map/add | solution.py:109
  78.3 1.0 fusion.68
  79.3 1.9 collective-permute-start.4
  81.3 8.3 %collective-permute-start.5 = (f32[2,1,2816]{2,1,0:T(1,128)S(1)}, f32[2,1,2816]{2,1,0:T(1,128)S(1)}, u32[]{:S(2)}, u32[]{:S(2)}) collective-permute-start(f32[2,1,2816]{2,1,0:T(1,128)S(1)} %get-tuple-element.48), channel_id=1, source_target_pairs={{1,0},{2,1},{3,2},{4,3},{5,4},{6,5},{7,6},{8,7},{9,8},{10,9},{11,1... | collective-permute-start | bytes 67592 | tf_op jit(solution)/shard_map/ppermute | solution.py:18
  89.6 0.0 collective-permute-done.4
  89.6 0.7 collective-permute-done.5
  90.3 0.0 copy-done.2
  90.3 0.0 copy-done.3
  90.3 0.0 copy-done.4
  90.3 0.0 copy-done.5
  90.3 12.9 %fusion.22 = (f32[2,128,2816]{2,1,0:T(8,128)}, f32[2,128,2816]{2,1,0:T(8,128)}) fusion(f32[2,128,2816]{2,1,0:T(8,128)} %get-tuple-element.40, f32[2,128,2816]{2,1,0:T(8,128)} %fusion.13, f32[2,128,2816]{2,1,0:T(8,128)S(1)} %copy-done.5, f32[2,128,2816]{2,1,0:T(8,128)S(1)} %copy-done.4, f32[2,1,2816]{2,1,0:T(1,128)S(1)} %collective-permute-done.5, ...), kind=kLoop, calls=%fused_computation.42 | loop fusion | flops 23068672 | bytes 28880896 | tf_op jit(solution)/shard_map/mul | solution.py:76
  103.3 5.6 %copy.39 = f32[2,128,2816]{2,0,1:T(2,128)} copy(f32[2,128,2816]{2,1,0:T(8,128)} %get-tuple-element.45) | data formatting | bytes 5767168 | tf_op jit(solution)/shard_map/mul | solution.py:76
  108.9 0.0 copy-start.8
  108.9 9.1 %all-to-all-start = ((f32[2,128,2816]{2,0,1:T(2,128)}), f32[2,128,2816]{2,0,1:T(2,128)}, u32[]{:S(2)}, u32[]{:S(2)}) async-start(f32[2,128,2816]{2,0,1:T(2,128)} %copy.39), calls=%async_computation | async-start | bytes 5767168 | tf_op jit(solution)/shard_map/all_to_all | solution.py:132
  118.0 0.0 copy-done.8
  118.0 3.8 %copy.42 = f32[2,128,2816]{2,0,1:T(2,128)} copy(f32[2,128,2816]{2,1,0:T(8,128)S(1)} %copy-done.8) | data formatting | bytes 5767168 | tf_op jit(solution)/shard_map/div | solution.py:130
  121.8 28.5 %all-to-all-done = f32[2,128,2816]{2,0,1:T(2,128)} async-done(((f32[2,128,2816]{2,0,1:T(2,128)}), f32[2,128,2816]{2,0,1:T(2,128)}, u32[]{:S(2)}, u32[]{:S(2)}) %all-to-all-start) | async-done | bytes 2883616 | tf_op jit(solution)/shard_map/all_to_all | solution.py:132
  150.3 5.6 %all-to-all-start.1 = ((f32[2,128,2816]{2,0,1:T(2,128)}), f32[2,128,2816]{2,0,1:T(2,128)S(1)}, u32[]{:S(2)}, u32[]{:S(2)}) async-start(f32[2,128,2816]{2,0,1:T(2,128)} %copy.42), calls=%async_computation.1 | async-start | bytes 5767168 | tf_op jit(solution)/shard_map/all_to_all | solution.py:133
  155.9 2.0 copy.40
  157.9 1.8 copy.41
  159.7 28.4 %all-to-all-done.1 = f32[2,128,2816]{2,0,1:T(2,128)S(1)} async-done(((f32[2,128,2816]{2,0,1:T(2,128)}), f32[2,128,2816]{2,0,1:T(2,128)S(1)}, u32[]{:S(2)}, u32[]{:S(2)}) %all-to-all-start.1) | async-done | bytes 2883616 | tf_op jit(solution)/shard_map/all_to_all | solution.py:133
  188.1 0.2 copy.43
  188.3 0.0 copy-start.7
  188.3 0.2 copy.44
  188.5 1.6 copy-done.7
  190.1 0.6 fusion.51
  190.7 0.6 add_dynamic-update-slice_fusion
  191.3 0.1 constant_dynamic-update-slice_fusion.5
  191.4 0.1 constant_dynamic-update-slice_fusion.3
  191.5 0.1 constant_dynamic-update-slice_fusion.1
  191.6 36.6 %all_to_all.54 = f32[8,32,2816]{2,1,0:T(8,128)S(1)} all-to-all(f32[8,32,2816]{2,1,0:T(8,128)S(1)} %constant_dynamic-update-slice_fusion), channel_id=1, replica_groups=mesh['layer'=4,'tile'=32] {'layer'}, dimensions={0} | all-to-all | bytes 5767168 | tf_op jit(solution)/shard_map/all_to_all | solution.py:135
  228.2 1.8 copy.45
  (5 shorter events, 0.1 us)
Async XLA Ops:
  2.3 6.7 %copy-start.6 = (f32[2,128,2816]{2,1,0:T(8,128)S(1)}, f32[2,128,2816]{2,1,0:T(8,128)}, u32[]{:S(2)}) copy-start(f32[2,128,2816]{2,1,0:T(8,128)} %param.10) | copy-start | bytes 8650756
  9.1 9.8 %collective-permute-start = (f32[2,2,1,2816]{3,2,1,0:T(1,128)S(1)}, f32[2,2,1,2816]{3,2,1,0:T(1,128)S(1)}, u32[]{:S(2)}, u32[]{:S(2)}) collective-permute-start(f32[2,2,1,2816]{3,2,1,0:T(1,128)S(1)} %get-tuple-element.43), channel_id=1, source_target_pairs={{0,1},{1,2},{2,3},{3,4},{4,5},{5,6},{6,7},{7,8},{8,9},{9,10},{10,1... | collective-permute-start | bytes 135176 | tf_op jit(solution)/shard_map/ppermute | solution.py:15
  12.3 7.7 %collective-permute-start.1 = (f32[2,2,1,2816]{3,2,1,0:T(1,128)S(1)}, f32[2,2,1,2816]{3,2,1,0:T(1,128)S(1)}, u32[]{:S(2)}, u32[]{:S(2)}) collective-permute-start(f32[2,2,1,2816]{3,2,1,0:T(1,128)S(1)} %get-tuple-element.44), channel_id=1, source_target_pairs={{1,0},{2,1},{3,2},{4,3},{5,4},{6,5},{7,6},{8,7},{9,8},{10,9},{11,1... | collective-permute-start | bytes 135176 | tf_op jit(solution)/shard_map/ppermute | solution.py:18
  22.8 2.5 %copy-start = (f32[2,130,2816]{2,1,0:T(8,128)}, f32[2,130,2816]{2,1,0:T(8,128)S(1)}, u32[]{:S(2)}) copy-start(f32[2,130,2816]{2,1,0:T(8,128)S(1)} %get-tuple-element.41) | copy-start | bytes 8785924
  22.8 3.4 %copy-start.1 = (f32[2,130,2816]{2,1,0:T(8,128)}, f32[2,130,2816]{2,1,0:T(8,128)S(1)}, u32[]{:S(2)}) copy-start(f32[2,130,2816]{2,1,0:T(8,128)S(1)} %get-tuple-element.42) | copy-start | bytes 8785924
  52.3 10.1 %collective-permute-start.2 = (f32[2,1,2816]{2,1,0:T(1,128)S(1)}, f32[2,1,2816]{2,1,0:T(1,128)S(1)}, u32[]{:S(2)}, u32[]{:S(2)}) collective-permute-start(f32[2,1,2816]{2,1,0:T(1,128)S(1)} %get-tuple-element.49), channel_id=1, source_target_pairs={{0,1},{1,2},{2,3},{3,4},{4,5},{5,6},{6,7},{7,8},{8,9},{9,10},{10,1... | collective-permute-start | bytes 67592 | tf_op jit(solution)/shard_map/ppermute | solution.py:15
  54.2 9.1 %collective-permute-start.3 = (f32[2,1,2816]{2,1,0:T(1,128)S(1)}, f32[2,1,2816]{2,1,0:T(1,128)S(1)}, u32[]{:S(2)}, u32[]{:S(2)}) collective-permute-start(f32[2,1,2816]{2,1,0:T(1,128)S(1)} %get-tuple-element.50), channel_id=1, source_target_pairs={{1,0},{2,1},{3,2},{4,3},{5,4},{6,5},{7,6},{8,7},{9,8},{10,9},{11,1... | collective-permute-start | bytes 67592 | tf_op jit(solution)/shard_map/ppermute | solution.py:18
  63.3 27.0 %copy-start.2 = (s32[2,128,2816]{2,1,0:T(8,128)S(1)}, s32[2,128,2816]{2,1,0:T(8,128)}, u32[]{:S(2)}) copy-start(s32[2,128,2816]{2,1,0:T(8,128)} %param.8) | copy-start | bytes 8650756
  63.3 27.0 %copy-start.3 = (f32[2,128,2816]{2,1,0:T(8,128)S(1)}, f32[2,128,2816]{2,1,0:T(8,128)}, u32[]{:S(2)}) copy-start(f32[2,128,2816]{2,1,0:T(8,128)} %get-tuple-element.37) | copy-start | bytes 8650756
  63.3 27.0 %copy-start.4 = (f32[2,128,2816]{2,1,0:T(8,128)S(1)}, f32[2,128,2816]{2,1,0:T(8,128)}, u32[]{:S(2)}) copy-start(f32[2,128,2816]{2,1,0:T(8,128)} %get-tuple-element.38) | copy-start | bytes 8650756
  63.3 27.0 %copy-start.5 = (f32[2,128,2816]{2,1,0:T(8,128)S(1)}, f32[2,128,2816]{2,1,0:T(8,128)}, u32[]{:S(2)}) copy-start(f32[2,128,2816]{2,1,0:T(8,128)} %get-tuple-element.39) | copy-start | bytes 8650756
  79.3 10.3 %collective-permute-start.4 = (f32[2,1,2816]{2,1,0:T(1,128)S(1)}, f32[2,1,2816]{2,1,0:T(1,128)S(1)}, u32[]{:S(2)}, u32[]{:S(2)}) collective-permute-start(f32[2,1,2816]{2,1,0:T(1,128)S(1)} %get-tuple-element.47), channel_id=1, source_target_pairs={{0,1},{1,2},{2,3},{3,4},{4,5},{5,6},{6,7},{7,8},{8,9},{9,10},{10,1... | collective-permute-start | bytes 67592 | tf_op jit(solution)/shard_map/ppermute | solution.py:15
  81.3 9.1 %collective-permute-start.5 = (f32[2,1,2816]{2,1,0:T(1,128)S(1)}, f32[2,1,2816]{2,1,0:T(1,128)S(1)}, u32[]{:S(2)}, u32[]{:S(2)}) collective-permute-start(f32[2,1,2816]{2,1,0:T(1,128)S(1)} %get-tuple-element.48), channel_id=1, source_target_pairs={{1,0},{2,1},{3,2},{4,3},{5,4},{6,5},{7,6},{8,7},{9,8},{10,9},{11,1... | collective-permute-start | bytes 67592 | tf_op jit(solution)/shard_map/ppermute | solution.py:18
  108.9 9.1 %copy-start.8 = (f32[2,128,2816]{2,1,0:T(8,128)S(1)}, f32[2,128,2816]{2,1,0:T(8,128)}, u32[]{:S(2)}) copy-start(f32[2,128,2816]{2,1,0:T(8,128)} %get-tuple-element.46) | copy-start | bytes 8650756
  108.9 41.4 %all-to-all-start = ((f32[2,128,2816]{2,0,1:T(2,128)}), f32[2,128,2816]{2,0,1:T(2,128)}, u32[]{:S(2)}, u32[]{:S(2)}) async-start(f32[2,128,2816]{2,0,1:T(2,128)} %copy.39), calls=%async_computation | async-start | bytes 5767168 | tf_op jit(solution)/shard_map/all_to_all | solution.py:132
  150.3 37.8 %all-to-all-start.1 = ((f32[2,128,2816]{2,0,1:T(2,128)}), f32[2,128,2816]{2,0,1:T(2,128)S(1)}, u32[]{:S(2)}, u32[]{:S(2)}) async-start(f32[2,128,2816]{2,0,1:T(2,128)} %copy.42), calls=%async_computation.1 | async-start | bytes 5767168 | tf_op jit(solution)/shard_map/all_to_all | solution.py:133
  188.3 1.8 copy-start.7
where the time goes:
time: 234 us; the launch traced here: 230 us
  other arithmetic  61.5 us (26%)
  waiting for transfers between devices  59.6 us (25%)
  starting transfers between devices  44.8 us (19%)
  blocking collectives  36.6 us (16%)
  local copies, waits for them, and re-layouts  26.6 us (11%)
    all_to_all x1, blocking collectives, local(): lax.all_to_all(solved, 'layer', split_axis=0, concat_axis=1, tiled=True)  36.6 us
    all_to_all x1, waiting for transfers between devices, local(): lax.all_to_all(heat, 'layer', split_axis=1, concat_axis=0, tiled=True)  28.5 us
    all_to_all x1, waiting for transfers between devices, local(): lax.all_to_all(vertical_flux, 'layer', split_axis=1, concat_axis=0, tiled...  28.4 us
    add x1, other arithmetic, local(): drop_one = drop_prior + step_one  23.3 us
    ppermute x3, starting transfers between devices, with_halo(): lax.ppermute(lax.slice_in_dim(block, 0, width, axis=dim), axis, backward)  23.1 us
    add x1, other arithmetic, chebyshev_tail(): return drop_one + step_two  15 us
    mul x1, other arithmetic, joule(): return 0.1 * (0.5 * heat + shunt * own * own)  12.9 us
    all_to_all x1, starting transfers between devices, local(): lax.all_to_all(heat, 'layer', split_axis=1, concat_axis=0, tiled=True)  9.1 us
  transfers between devices with their start and end apart: 8, of which 5 were waited for; matrix products, arithmetic and copies ran while one was open for 3% of the time, Pallas kernels for 0%

commit v1 on v0

v1 whole, which is shorter than its diff:
```python
import functools

import jax
import jax.numpy as jnp
from jax import lax
from jax.experimental import pallas as pl
from jax.experimental.pallas import tpu as pltpu
from jax.sharding import PartitionSpec as P

MESH = pl.DeviceIdType.MESH
F32 = jnp.float32
ROWS = 128
LANES = 128
PAD = 8
HALF_WIDTH = 0.9
RHO_ONE = 0.9
RHO_TWO = 1.0 / (2.0 / HALF_WIDTH - RHO_ONE)
KEEP = RHO_TWO * RHO_ONE
GAIN = 2.0 * RHO_TWO / HALF_WIDTH
ALONG_ROWS = (1.0, 0.25)
ALONG_COLS = (0.25, 1.0)


def rcp(x):
    return pltpu.reciprocal(x, approx=True)


def kernel(
    nt, nl, tiles,
    load_h, cls_h, via_h, temp_h, x0_h, table,
    drop_h, rise_h,
    load, cls, via, temp, x0, x1, x2, res, shunt, inv, east, south, flux, tabs,
    ra, wa, rb, wb, pbuf, nbuf, pin, nin, mid_p, mid_n, t_own, t_far, t_in, t_out,
    h0s, h0r, h1s, h1r, h2s, h2r,
    in_sem, out_sem, hs_sem, hr_sem,
    p_ss, p_rs, n_ss, n_rs, mp_ss, mp_rs, mn_ss, mn_rs, mt_ss, mt_rs, t_ss, t_rs,
):
    d = lax.axis_index("layer")
    tile = lax.axis_index("tile")
    half = tiles // 2
    low = d < nl // 2
    outer = jnp.logical_or(d == 0, d == nl - 1)
    inner = jnp.logical_not(outer)
    lane = lax.broadcasted_iota(jnp.int32, (8, LANES), 1)
    heats = temp

    def order(i):
        j = i + jnp.where(low, half, 0)
        return jnp.where(j >= tiles, j - tiles, j)

    def cols(j):
        return pl.ds(pl.multiple_of(j * LANES, LANES), LANES)

    def fetch(k, j):
        src, dst = (
            (temp_h, temp), (via_h, via), (cls_h, cls), (x0_h, x0), (load_h, load)
        )[k]
        target = dst.at[:, j, pl.ds(PAD, ROWS), :] if k == 3 else dst.at[:, j]
        return pltpu.make_async_copy(src.at[:, :, cols(j)], target, in_sem.at[k, j])

    for ks in ((0, 1), (2,), (3,), (4,)):
        def start_in(i, carry, ks=ks):
            for k in ks:
                fetch(k, order(i)).start()
            return carry
        lax.fori_loop(0, tiles, start_in, 0)

    barrier = pltpu.get_barrier_semaphore()

    def greet(cond, where):
        @pl.when(cond)
        def _():
            pl.semaphore_signal(barrier, inc=1, device_id=where, device_id_type=MESH)

    north_ok = tile > 0
    south_ok = tile < nt - 1
    greet(north_ok, (d, tile - 1))
    greet(south_ok, (d, tile + 1))
    greet(d > 0, (d - 1, tile))
    greet(d < nl - 1, (d + 1, tile))

    tabs[...] = jnp.ones_like(tabs)
    for l in range(2):
        tabs[l, 0:1, 0:16] = 0.5 / table[l : l + 1, :]
        east[l, 0] = jnp.zeros((ROWS, LANES), F32)
        x0[l, tiles] = jnp.zeros((ROWS + 2 * PAD, LANES), F32)
        x1[l, tiles] = jnp.zeros((ROWS + 2 * PAD, LANES), F32)
        x2[l, tiles] = jnp.zeros((ROWS + 2 * PAD, LANES), F32)
        res[l, tiles] = jnp.ones((ROWS + 2 * PAD, LANES), F32)

    @pl.when(tile == 0)
    def _():
        h0r[0, 0:2] = jnp.ones((2, 24, LANES), F32)
        h0r[0, 2:4] = jnp.zeros((2, 24, LANES), F32)
        h1r[0] = jnp.zeros((2, 24, LANES), F32)
        h2r[0] = jnp.zeros((2, 24, LANES), F32)

    @pl.when(tile == nt - 1)
    def _():
        h0r[1, 0:2] = jnp.ones((2, 24, LANES), F32)
        h0r[1, 2:4] = jnp.zeros((2, 24, LANES), F32)
        h1r[1] = jnp.zeros((2, 24, LANES), F32)
        h2r[1] = jnp.zeros((2, 24, LANES), F32)

    pl.semaphore_wait(
        barrier,
        north_ok.astype(jnp.int32) + south_ok.astype(jnp.int32)
        + (d > 0).astype(jnp.int32) + (d < nl - 1).astype(jnp.int32),
    )

    def halo(stage, side, arriving=False):
        up = (side == 0) != arriving
        send, recv = ((h0s, h0r), (h1s, h1r), (h2s, h2r))[stage]
        return pltpu.make_async_remote_copy(
            src_ref=send.at[side], dst_ref=recv.at[1 - side],
            send_sem=hs_sem.at[stage, side], recv_sem=hr_sem.at[stage, 1 - side],
            device_id=(d, tile - 1 if up else tile + 1), device_id_type=MESH,
        )

    def halo_send(stage, fields):
        send = (h0s, h1s, h2s)[stage]

        def pack(j, carry):
            for f, ref in enumerate(fields):
                for l in range(2):
                    send[0, 2 * f + l, pl.ds(j, 1), :] = ref[l, j, PAD : PAD + 1, :]
                    send[1, 2 * f + l, pl.ds(j, 1), :] = ref[l, j, PAD + ROWS - 1 : PAD + ROWS, :]
            return carry

        lax.fori_loop(0, tiles, pack, 0)
        for side, cond in ((0, north_ok), (1, south_ok)):
            @pl.when(cond)
            def _():
                halo(stage, side).start()

    def halo_recv(stage, fields):
        recv = (h0r, h1r, h2r)[stage]
        for side, cond in ((0, north_ok), (1, south_ok)):
            @pl.when(cond)
            def _():
                halo(stage, 1 - side, True).wait_recv()

        def unpack(j, carry):
            for f, ref in enumerate(fields):
                for l in range(2):
                    ref[l, j, PAD - 1 : PAD, :] = recv[0, 2 * f + l, pl.ds(j, 1), :]
                    ref[l, j, PAD + ROWS : PAD + ROWS + 1, :] = recv[1, 2 * f + l, pl.ds(j, 1), :]
            return carry

        lax.fori_loop(0, tiles, unpack, 0)

    def halo_done(stage):
        for side, cond in ((0, north_ok), (1, south_ok)):
            @pl.when(cond)
            def _():
                halo(stage, side).wait_send()

    def toward(i):
        return (jnp.where(low, d + 1, d - 1), tile)

    def away(i):
        return (jnp.where(low, jnp.where(d == 0, d + 1, d - 1), jnp.where(d == nl - 1, d - 1, d + 1)), tile)

    def remote(src, dst, ss, rs, j, where):
        return pltpu.make_async_remote_copy(
            src_ref=src.at[j], dst_ref=dst.at[j], send_sem=ss.at[j], recv_sem=rs.at[j],
            device_id=where, device_id_type=MESH,
        )

    def p_in(i):
        return remote(pbuf, pin, p_ss, p_rs, i, toward(i))

    def n_in(i):
        return remote(nbuf, nin, n_ss, n_rs, i, toward(i))

    def p_mid(i):
        return remote(pbuf, mid_p, mp_ss, mp_rs, i, toward(i))

    def n_mid(i):
        return remote(nbuf, mid_n, mn_ss, mn_rs, i, toward(i))

    def t_mid(i):
        return remote(t_own, t_far, mt_ss, mt_rs, i, toward(i))

    def t_back(i):
        return remote(t_out, t_in, t_ss, t_rs, i, away(i))

    def vertical(l, j, rows):
        up = 1.0 + 4.0 * via[l, j, rows, :].astype(F32)
        return up * rcp(0.95 + 0.002 * temp[l, j, rows, :])

    def matrix(role, i):
        j = order(i)
        for r in range(0, ROWS, 32):
            rows = pl.ds(r, 32)
            v0 = vertical(0, j, rows)
            v1 = vertical(1, j, rows)
            if role == 0:
                da = jnp.full((32, LANES), 0.2, F32)
            elif role == 1:
                da = 0.2 + pin[i, rows, :]
            elif role == 2:
                got = pin[i, rows, :]
                rr = rcp(got + v1)
                wi = v1 * rr
                da = 0.2 + wi * got
                rb[i, rows, :] = rr
                wb[i, rows, :] = wi
            else:
                da = 0.2 + v1
            r_a = rcp(da + v0)
            w_a = v0 * r_a
            ra[i, rows, :] = r_a
            wa[i, rows, :] = w_a
            db = 0.2 + w_a * da
            if role < 2:
                r_b = rcp(db + v1)
                w_b = v1 * r_b
                rb[i, rows, :] = r_b
                wb[i, rows, :] = w_b
                db = w_b * db
            pbuf[i, rows, :] = db

    def outer_matrix(role):
        def body(i, carry):
            fetch(0, order(i)).wait()
            fetch(1, order(i)).wait()
            matrix(role, i)
            p_in(i).start()
            return carry
        lax.fori_loop(0, tiles, body, 0)

    def inner_matrix(role):
        def body(i, carry):
            fetch(1, order(i)).wait()
            p_in(i).wait_recv()
            matrix(role, i)

            @pl.when(i < half)
            def _():
                p_mid(i).start()
            return carry
        lax.fori_loop(0, tiles, body, 0)

    @pl.when(d == 0)
    def _():
        outer_matrix(0)

    @pl.when(d == nl - 1)
    def _():
        outer_matrix(3)

    def resist(i, carry):
        j = order(i)

        @pl.when(inner)
        def _():
            fetch(0, j).wait()
        fetch(2, j).wait()
        for l in range(2):
            look = jnp.broadcast_to(tabs[l, 0:1, :], (8, LANES))
            for r in range(0, ROWS, 8):
                base = jnp.take_along_axis(look, cls[l, j, pl.ds(r, 8), :], axis=1)
                res[l, j, pl.ds(PAD + r, 8), :] = base * (0.9025 + 0.0039 * temp[l, j, pl.ds(r, 8), :])
        fetch(3, j).wait()
        return carry

    lax.fori_loop(0, tiles, resist, 0)
    halo_send(0, (res, x0))

    @pl.when(d == 1)
    def _():
        inner_matrix(1)

    @pl.when(d == 2)
    def _():
        inner_matrix(2)

    def next_col(ref, l, j, rows, own, n):
        mixed = jnp.where(lane_of(n) == 0, ref[l, j + 1, rows, :], own)
        return pltpu.roll(mixed, LANES - 1, 1)

    def lane_of(n):
        return lax.broadcasted_iota(jnp.int32, (n, LANES), 1)

    def prev_col(before, own, n):
        return pltpu.roll(jnp.where(lane_of(n) == LANES - 1, before, own), 1, 1)

    def apply(xref, l, j, r, n, e, s, s_up, g):
        at = pl.ds(PAD + r, n)
        x = xref[l, j, at, :]
        fe = e * (x - next_col(xref, l, j, at, x, n))
        before = flux[l, pl.ds(r, n), :]
        flux[l, pl.ds(r, n), :] = fe
        fs = s * (x - xref[l, j, pl.ds(PAD + r + 1, n), :])
        fn = s_up * (xref[l, j, pl.ds(PAD + r - 1, n), :] - x)
        return x, (fe - prev_col(before, fe, n)) + (fs - fn) + g * x

    def first(j, l, r, n):
        at = pl.ds(PAD + r, n)
        rows = pl.ds(r, n)
        own = res[l, j, at, :]
        e = ALONG_COLS[l] * rcp(own + next_col(res, l, j, at, own, n))
        last = jnp.logical_and(lane_of(n) == LANES - 1, j == tiles - 1)
        e = jnp.where(last, 0.0, e)
        e_before = prev_col(east[l, j, rows, :], e, n)
        east[l, j + 1, rows, :] = e
        s = ALONG_ROWS[l] * rcp(own + res[l, j, pl.ds(PAD + r + 1, n), :])
        s_up = ALONG_ROWS[l] * rcp(own + res[l, j, pl.ds(PAD + r - 1, n), :])
        row = lax.broadcasted_iota(jnp.int32, (n, LANES), 0)
        if r == 0:
            s_up = jnp.where(jnp.logical_and(row == 0, tile == 0), 0.0, s_up)
            south[l, j, PAD - 1 : PAD, :] = s_up[0:1, :]
        if r + n == ROWS:
            s = jnp.where(jnp.logical_and(row == n - 1, tile == nt - 1), 0.0, s)
        south[l, j, at, :] = s
        g = (0.025 + 0.25 * via[l, j, rows, :].astype(F32)) * rcp(own)
        shunt[l, j, rows, :] = g
        iv = rcp(e + e_before + s + s_up + g)
        inv[l, j, rows, :] = iv
        x, ax = apply(x0, l, j, r, n, e, s, s_up, g)
        x1[l, j, at, :] = x + (load[l, j, rows, :] - ax) * iv

    def edges(l, j, r, n):
        return (
            east[l, j + 1, pl.ds(r, n), :],
            south[l, j, pl.ds(PAD + r, n), :],
            south[l, j, pl.ds(PAD + r - 1, n), :],
            shunt[l, j, pl.ds(r, n), :],
        )

    def second(j, l, r, n):
        at = pl.ds(PAD + r, n)
        rows = pl.ds(r, n)
        e, s, s_up, g = edges(l, j, r, n)
        x, ax = apply(x1, l, j, r, n, e, s, s_up, g)
        change = (load[l, j, rows, :] - ax) * inv[l, j, rows, :]
        x2[l, j, at, :] = x + (KEEP * (x - x0[l, j, at, :]) + GAIN * change)

    def heat(j, l, r, n):
        at = pl.ds(PAD + r, n)
        e, s, s_up, g = edges(l, j, r, n)
        x = x2[l, j, at, :]
        de = x - next_col(x2, l, j, at, x, n)
        ds_ = x - x2[l, j, pl.ds(PAD + r + 1, n), :]
        dn = x2[l, j, pl.ds(PAD + r - 1, n), :] - x
        fe = e * de * de
        east_before = east[l, j, pl.ds(r, n), :]
        xb = x2[l, j - 1 + jnp.where(j == 0, 1, 0), at, :]
        dw = x - prev_col(xb, x, n)
        ew = prev_col(east_before, e, n)
        sum_ = (fe + ew * dw * dw) + (s * ds_ * ds_ + s_up * dn * dn)
        heats[l, j, pl.ds(r, n), :] = 0.05 * sum_ + (0.1 * g) * x * x

    def sweep(fn, parts):
        def zero(l):
            flux[l] = jnp.zeros((ROWS, LANES), F32)
        for l in range(2):
            zero(l)

        def body(j, carry):
            for l in range(2):
                for r, n in parts:
                    fn(j, l, r, n)
            return carry
        lax.fori_loop(0, tiles, body, 0)

    rim = ((0, 8), (ROWS - 8, 8))

    def wait_load(j, carry):
        fetch(4, j).wait()
        return carry
    lax.fori_loop(0, tiles, wait_load, 0)
    sweep(first, ((8, 24), (32, 24)))
    halo_recv(0, (res, x0))
    sweep(first, rim)
    halo_send(1, (x1,))
    sweep(first, ((56, 32), (88, 32)))
    halo_recv(1, (x1,))
    sweep(second, rim)
    halo_send(2, (x2,))
    sweep(second, ((8, 32), (40, 32), (72, 24), (96, 24)))
    halo_recv(2, (x2,))

    def drop_out(j):
        return pltpu.make_async_copy(
            x2.at[:, j, pl.ds(PAD, ROWS), :], drop_h.at[:, :, cols(j)], out_sem.at[0, j]
        )

    def rise_out(j):
        return pltpu.make_async_copy(heats.at[:, j], rise_h.at[:, :, cols(j)], out_sem.at[1, j])

    def right_side(role, i):
        j = order(i)
        a, b = (0, 1) if role < 2 else (1, 0)
        for r in range(0, ROWS, 32):
            rows = pl.ds(r, 32)
            na = heats[a, j, rows, :]
            if role == 1:
                na = na + nin[i, rows, :]
                heats[a, j, rows, :] = na
            elif role == 2:
                na = na + wb[i, rows, :] * nin[i, rows, :]
                heats[a, j, rows, :] = na
            nb = heats[b, j, rows, :] + wa[i, rows, :] * na
            heats[b, j, rows, :] = nb
            nbuf[i, rows, :] = wb[i, rows, :] * nb if role < 2 else nb

    def inner_right(i):
        n_in(i).wait_recv()

        @pl.when(d == 1)
        def _():
            right_side(1, i)

        @pl.when(d == 2)
        def _():
            right_side(2, i)

        @pl.when(i < half)
        def _():
            n_mid(i).start()

    def heat_step(i, carry):
        j = order(i)
        drop_out(j).start()
        for l in range(2):
            for r in range(0, ROWS, 32):
                heat(j, l, r, 32)

        @pl.when(d == 0)
        def _():
            right_side(0, i)

        @pl.when(d == nl - 1)
        def _():
            right_side(3, i)

        @pl.when(outer)
        def _():
            n_in(i).start()

        @pl.when(jnp.logical_and(inner, i >= 2))
        def _():
            inner_right(i - 2)
        return carry

    lax.fori_loop(0, tiles, heat_step, 0)

    def back(role, i):
        j = order(i)
        a, b = (0, 1) if role < 2 else (1, 0)
        for r in range(0, ROWS, 32):
            rows = pl.ds(r, 32)
            tin = t_in[i, rows, :]
            tb = heats[b, j, rows, :] * rb[i, rows, :] + wb[i, rows, :] * tin if role < 2 else tin
            ta = heats[a, j, rows, :] * ra[i, rows, :] + wa[i, rows, :] * tb
            heats[b, j, rows, :] = tb
            heats[a, j, rows, :] = ta
            if role == 1:
                t_out[i, rows, :] = ta
            elif role == 2:
                t_out[i, rows, :] = rb[i, rows, :] * nin[i, rows, :] + wb[i, rows, :] * ta
        rise_out(j).start()

    def inner_back(i):
        @pl.when(d == 1)
        def _():
            back(1, i)

        @pl.when(d == 2)
        def _():
            back(2, i)
        t_back(i).start()

    @pl.when(inner)
    def _():
        inner_right(tiles - 2)
        inner_right(tiles - 1)

        def own(k, carry):
            i = half + k
            p_mid(k).wait_recv()
            n_mid(k).wait_recv()
            for r in range(0, ROWS, 32):
                rows = pl.ds(r, 32)
                t4 = (nbuf[i, rows, :] + mid_n[k, rows, :]) * rcp(pbuf[i, rows, :] + mid_p[k, rows, :])
                t_own[k, rows, :] = t4
                t_in[i, rows, :] = t4
            t_mid(k).start()
            inner_back(i)
            return carry
        lax.fori_loop(0, half, own, 0)

        def far(k, carry):
            t_mid(k).wait_recv()
            t_in[k] = t_far[k]
            inner_back(k)
            return carry
        lax.fori_loop(0, half, far, 0)

    @pl.when(outer)
    def _():
        def last(k, carry):
            i = k + half
            i = jnp.where(i >= tiles, i - tiles, i)
            t_back(i).wait_recv()

            @pl.when(d == 0)
            def _():
                back(0, i)

            @pl.when(d == nl - 1)
            def _():
                back(3, i)
            return carry
        lax.fori_loop(0, tiles, last, 0)

    for stage in range(3):
        halo_done(stage)

    def drain(i, carry):
        drop_out(i).wait()
        rise_out(i).wait()

        @pl.when(outer)
        def _():
            p_in(i).wait_send()
            n_in(i).wait_send()

        @pl.when(inner)
        def _():
            t_back(i).wait_send()

        @pl.when(jnp.logical_and(inner, i < half))
        def _():
            p_mid(i).wait_send()
            n_mid(i).wait_send()
            t_mid(i).wait_send()
        return carry
    lax.fori_loop(0, tiles, drain, 0)


def local(nt, nl, load_current, metal_class, via_mask, temp_prior, drop_prior, class_conductance):
    tiles = load_current.shape[2] // LANES
    half = tiles // 2
    wide = ROWS + 2 * PAD
    shape = jax.ShapeDtypeStruct(load_current.shape, F32)
    vm = pltpu.VMEM
    dma = pltpu.SemaphoreType.DMA
    field = vm((2, tiles, ROWS, LANES), F32)
    padded = vm((2, tiles + 1, wide, LANES), F32)
    column = vm((tiles, ROWS, LANES), F32)
    part = vm((half, ROWS, LANES), F32)
    return pl.pallas_call(
        functools.partial(kernel, nt, nl, tiles),
        out_shape=(shape, shape),
        in_specs=[pl.BlockSpec(memory_space=pl.ANY)] * 5 + [pl.BlockSpec(memory_space=pltpu.VMEM)],
        out_specs=[pl.BlockSpec(memory_space=pl.ANY)] * 2,
        scratch_shapes=[
            field,
            vm((2, tiles, ROWS, LANES), jnp.int32),
            vm((2, tiles, ROWS, LANES), jnp.int32),
            field,
            padded, padded, padded, padded,
            field, field,
            vm((2, tiles + 1, ROWS, LANES), F32),
            vm((2, tiles, ROWS + PAD, LANES), F32),
            vm((2, ROWS, LANES), F32),
            vm((2, 8, LANES), F32),
            column, column, column, column,
            column, column, column, column,
            part, part, part, part,
            column, column,
            vm((2, 4, 24, LANES), F32), vm((2, 4, 24, LANES), F32),
            vm((2, 2, 24, LANES), F32), vm((2, 2, 24, LANES), F32),
            vm((2, 2, 24, LANES), F32), vm((2, 2, 24, LANES), F32),
            dma((5, tiles)), dma((2, tiles)), dma((3, 2)), dma((3, 2)),
            dma((tiles,)), dma((tiles,)), dma((tiles,)), dma((tiles,)),
            dma((half,)), dma((half,)), dma((half,)), dma((half,)),
            dma((half,)), dma((half,)), dma((tiles,)), dma((tiles,)),
        ],
        compiler_params=pltpu.CompilerParams(
            collective_id=0, has_side_effects=True, vmem_limit_bytes=63000000
        ),
        cost_estimate=pl.CostEstimate(flops=100000000, bytes_accessed=20200000, transcendentals=5000000),
    )(load_current, metal_class, via_mask, temp_prior, drop_prior, class_conductance)


def solution(mesh):
    in_specs = (
        P("layer", "tile", None),
        P("layer", "tile", None),
        P("layer", "tile", None),
        P("layer", "tile", None),
        P("layer", "tile", None),
        P("layer", None),
    )
    out_specs = (P("layer", "tile", None), P("layer", "tile", None))
    return jax.shard_map(
        functools.partial(local, mesh.shape["tile"], mesh.shape["layer"]),
        mesh=mesh, in_specs=in_specs, out_specs=out_specs, check_vma=False,
    )
```

time: 234 us -> 65.5 us (0.28); the launches traced: 230 us -> 65.4 us
  other arithmetic: 61.5 us -> 0 us
  waiting for transfers between devices: 59.6 us -> 0 us
  Pallas kernels: 0 us -> 59.4 us
  starting transfers between devices: 44.8 us -> 0 us
  blocking collectives: 36.6 us -> 0 us
  local copies, waits for them, and re-layouts: 26.6 us -> 5.31 us
    pallas_call x0 -> x1, Pallas kernels: none -> 59.4 us  [local(): pl.pallas_call(functools.partial(kernel, nt, nl, tiles), out_shape=(shape...]
    all_to_all x2 -> x0, waiting for transfers between devices: 56.9 us -> none  [the longest x1 28.5 us: local(): lax.all_to_all(heat, 'layer', split_axis=1, concat_axis=0, tiled=True)]
    add x2 -> x0, other arithmetic: 38.3 us -> none  [the longest x1 23.3 us: local(): drop_one = drop_prior + step_one]
    all_to_all x1 -> x0, blocking collectives: 36.6 us -> none  [local(): lax.all_to_all(solved, 'layer', split_axis=0, concat_axis=1, tiled=True)]
    ppermute x6 -> x0, starting transfers between devices: 30.2 us -> none  [the longest x3 23.1 us: with_halo(): lax.ppermute(lax.slice_in_dim(block, 0, width, axis=dim), axis, backward)]
    all_to_all x2 -> x0, starting transfers between devices: 14.7 us -> none  [the longest x1 9.1 us: local(): lax.all_to_all(heat, 'layer', split_axis=1, concat_axis=0, tiled=True)]
    mul x1 -> x0, other arithmetic: 12.9 us -> none  [joule(): return 0.1 * (0.5 * heat + shunt * own * own)]
    slice x5 -> x0, local copies, waits for them, and re-layouts: 7.47 us -> none  [the longest x2 2.08 us: with_halo(): lax.slice_in_dim(block, block.shape[dim] - width, None, axis=dim)]
  transfers between devices with their start and end apart: 8 -> 0, of which waited for: 5 -> 0; matrix products, arithmetic and copies ran while one was open for 3% -> 0% of each run, Pallas kernels for 0% -> 0%
where the time goes in v1:
time: 65.5 us; the launch traced here: 65.4 us
  Pallas kernels  59.4 us (91%)
  local copies, waits for them, and re-layouts  5.31 us (8%)
    pallas_call x1, Pallas kernels, local(): pl.pallas_call(functools.partial(kernel, nt, nl, tiles), out_shape=(shape...  59.4 us
    unnamed x4, local copies, waits for them, and re-layouts  5.31 us

profile of v1, /device:TPU:99, one launch (start us, length us, event | category | flops | bytes accessed | tf_op | source)
XLA Modules:
  0.0 65.4 jit_solution(15922980181524846059)
XLA Ops:
  0.6 59.4 %shard_map.77 = (f32[2,128,2816]{2,1,0:T(8,128)}, f32[2,128,2816]{2,1,0:T(8,128)}) custom-call(f32[2,128,2816]{2,1,0:T(8,128)} %load_h.1, s32[2,128,2816]{2,1,0:T(8,128)} %cls_h.1, s32[2,128,2816]{2,1,0:T(8,128)} %via_h.1, f32[2,128,2816]{2,1,0:T(8,128)} %temp_h.1, f32[2,128,2816]{2,1,0:T(8,128)} %x0_h.1, f32[2,16]{1,0:T(2,128)} %table.1), custom_call_target="tpu_custom_call" | custom-call | flops 100000000 | bytes 20200000 | tf_op jit(solution)/shard_map/pallas_call | solution.py:555
  60.1 0.0 copy-start
  60.1 3.7 %copy.10 = f32[2,128,2816]{2,1,0:T(8,128)} copy(f32[2,128,2816]{2,1,0:T(8,128)} %get-tuple-element.4) | data formatting | bytes 5767168
  63.8 0.0 copy-done
  63.8 1.6 %copy.11 = f32[2,128,2816]{2,1,0:T(8,128)} copy(f32[2,128,2816]{2,1,0:T(8,128)S(1)} %copy-done) | data formatting | bytes 5767168
Async XLA Ops:
  60.1 3.7 %copy-start = (f32[2,128,2816]{2,1,0:T(8,128)S(1)}, f32[2,128,2816]{2,1,0:T(8,128)}, u32[]{:S(2)}) copy-start(f32[2,128,2816]{2,1,0:T(8,128)} %get-tuple-element.5) | copy-start | bytes 8650756

commit v2 on v1

--- a/solution.py
+++ b/solution.py
@@ -29,7 +29,7 @@
     nt, nl, tiles,
     load_h, cls_h, via_h, temp_h, x0_h, table,
     drop_h, rise_h,
-    load, cls, via, temp, x0, x1, x2, res, shunt, inv, east, south, flux, tabs,
+    load, cls, via, temp, x0, x1, x2, res, shunt, inv, east, west, south, tabs,
     ra, wa, rb, wb, pbuf, nbuf, pin, nin, mid_p, mid_n, t_own, t_far, t_in, t_out,
     h0s, h0r, h1s, h1r, h2s, h2r,
     in_sem, out_sem, hs_sem, hr_sem,
@@ -41,7 +41,6 @@
     low = d < nl // 2
     outer = jnp.logical_or(d == 0, d == nl - 1)
     inner = jnp.logical_not(outer)
-    lane = lax.broadcasted_iota(jnp.int32, (8, LANES), 1)
     heats = temp
 
     def order(i):
@@ -82,11 +81,6 @@
     tabs[...] = jnp.ones_like(tabs)
     for l in range(2):
         tabs[l, 0:1, 0:16] = 0.5 / table[l : l + 1, :]
-        east[l, 0] = jnp.zeros((ROWS, LANES), F32)
-        x0[l, tiles] = jnp.zeros((ROWS + 2 * PAD, LANES), F32)
-        x1[l, tiles] = jnp.zeros((ROWS + 2 * PAD, LANES), F32)
-        x2[l, tiles] = jnp.zeros((ROWS + 2 * PAD, LANES), F32)
-        res[l, tiles] = jnp.ones((ROWS + 2 * PAD, LANES), F32)
 
     @pl.when(tile == 0)
     def _():
@@ -232,6 +226,7 @@
 
     def inner_matrix(role):
         def body(i, carry):
+            fetch(0, order(i)).wait()
             fetch(1, order(i)).wait()
             p_in(i).wait_recv()
             matrix(role, i)
@@ -250,12 +245,16 @@
     def _():
         outer_matrix(3)
 
+    @pl.when(d == 1)
+    def _():
+        inner_matrix(1)
+
+    @pl.when(d == 2)
+    def _():
+        inner_matrix(2)
+
     def resist(i, carry):
         j = order(i)
-
-        @pl.when(inner)
-        def _():
-            fetch(0, j).wait()
         fetch(2, j).wait()
         for l in range(2):
             look = jnp.broadcast_to(tabs[l, 0:1, :], (8, LANES))
@@ -268,43 +267,41 @@
     lax.fori_loop(0, tiles, resist, 0)
     halo_send(0, (res, x0))
 
-    @pl.when(d == 1)
-    def _():
-        inner_matrix(1)
-
-    @pl.when(d == 2)
-    def _():
-        inner_matrix(2)
-
-    def next_col(ref, l, j, rows, own, n):
-        mixed = jnp.where(lane_of(n) == 0, ref[l, j + 1, rows, :], own)
-        return pltpu.roll(mixed, LANES - 1, 1)
-
     def lane_of(n):
         return lax.broadcasted_iota(jnp.int32, (n, LANES), 1)
 
-    def prev_col(before, own, n):
-        return pltpu.roll(jnp.where(lane_of(n) == LANES - 1, before, own), 1, 1)
-
-    def apply(xref, l, j, r, n, e, s, s_up, g):
+    def next_col(ref, l, j, rows, own, n):
+        side = ref[l, jnp.where(j == tiles - 1, j, j + 1), rows, :]
+        return pltpu.roll(jnp.where(lane_of(n) == 0, side, own), LANES - 1, 1)
+
+    def prev_col(ref, l, j, rows, own, n):
+        side = ref[l, jnp.where(j == 0, j, j - 1), rows, :]
+        return pltpu.roll(jnp.where(lane_of(n) == LANES - 1, side, own), 1, 1)
+
+    def differences(xref, l, j, r, n):
         at = pl.ds(PAD + r, n)
         x = xref[l, j, at, :]
-        fe = e * (x - next_col(xref, l, j, at, x, n))
-        before = flux[l, pl.ds(r, n), :]
-        flux[l, pl.ds(r, n), :] = fe
-        fs = s * (x - xref[l, j, pl.ds(PAD + r + 1, n), :])
-        fn = s_up * (xref[l, j, pl.ds(PAD + r - 1, n), :] - x)
-        return x, (fe - prev_col(before, fe, n)) + (fs - fn) + g * x
+        return (
+            x,
+            x - next_col(xref, l, j, at, x, n),
+            x - prev_col(xref, l, j, at, x, n),
+            x - xref[l, j, pl.ds(PAD + r + 1, n), :],
+            x - xref[l, j, pl.ds(PAD + r - 1, n), :],
+        )
+
+    def apply(xref, l, j, r, n, e, w, s, s_up, g):
+        x, de, dw, ds_, dn = differences(xref, l, j, r, n)
+        return x, (e * de + w * dw) + (s * ds_ + s_up * dn) + g * x
 
     def first(j, l, r, n):
         at = pl.ds(PAD + r, n)
         rows = pl.ds(r, n)
         own = res[l, j, at, :]
+        lanes = lane_of(n)
         e = ALONG_COLS[l] * rcp(own + next_col(res, l, j, at, own, n))
-        last = jnp.logical_and(lane_of(n) == LANES - 1, j == tiles - 1)
-        e = jnp.where(last, 0.0, e)
-        e_before = prev_col(east[l, j, rows, :], e, n)
-        east[l, j + 1, rows, :] = e
+        e = jnp.where(jnp.logical_and(lanes == LANES - 1, j == tiles - 1), 0.0, e)
+        w = ALONG_COLS[l] * rcp(own + prev_col(res, l, j, at, own, n))
+        w = jnp.where(jnp.logical_and(lanes == 0, j == 0), 0.0, w)
         s = ALONG_ROWS[l] * rcp(own + res[l, j, pl.ds(PAD + r + 1, n), :])
         s_up = ALONG_ROWS[l] * rcp(own + res[l, j, pl.ds(PAD + r - 1, n), :])
         row = lax.broadcasted_iota(jnp.int32, (n, LANES), 0)
@@ -313,17 +310,20 @@
             south[l, j, PAD - 1 : PAD, :] = s_up[0:1, :]
         if r + n == ROWS:
             s = jnp.where(jnp.logical_and(row == n - 1, tile == nt - 1), 0.0, s)
+        g = (0.025 + 0.25 * via[l, j, rows, :].astype(F32)) * rcp(own)
+        iv = rcp((e + w) + (s + s_up) + g)
+        x, ax = apply(x0, l, j, r, n, e, w, s, s_up, g)
+        x1[l, j, at, :] = x + (load[l, j, rows, :] - ax) * iv
+        east[l, j, rows, :] = e
+        west[l, j, rows, :] = w
         south[l, j, at, :] = s
-        g = (0.025 + 0.25 * via[l, j, rows, :].astype(F32)) * rcp(own)
         shunt[l, j, rows, :] = g
-        iv = rcp(e + e_before + s + s_up + g)
         inv[l, j, rows, :] = iv
-        x, ax = apply(x0, l, j, r, n, e, s, s_up, g)
-        x1[l, j, at, :] = x + (load[l, j, rows, :] - ax) * iv
 
     def edges(l, j, r, n):
         return (
-            east[l, j + 1, pl.ds(r, n), :],
+            east[l, j, pl.ds(r, n), :],
+            west[l, j, pl.ds(r, n), :],
             south[l, j, pl.ds(PAD + r, n), :],
             south[l, j, pl.ds(PAD + r - 1, n), :],
             shunt[l, j, pl.ds(r, n), :],
@@ -332,38 +332,26 @@
     def second(j, l, r, n):
         at = pl.ds(PAD + r, n)
         rows = pl.ds(r, n)
-        e, s, s_up, g = edges(l, j, r, n)
-        x, ax = apply(x1, l, j, r, n, e, s, s_up, g)
+        x, ax = apply(x1, l, j, r, n, *edges(l, j, r, n))
         change = (load[l, j, rows, :] - ax) * inv[l, j, rows, :]
         x2[l, j, at, :] = x + (KEEP * (x - x0[l, j, at, :]) + GAIN * change)
 
     def heat(j, l, r, n):
-        at = pl.ds(PAD + r, n)
-        e, s, s_up, g = edges(l, j, r, n)
-        x = x2[l, j, at, :]
-        de = x - next_col(x2, l, j, at, x, n)
-        ds_ = x - x2[l, j, pl.ds(PAD + r + 1, n), :]
-        dn = x2[l, j, pl.ds(PAD + r - 1, n), :] - x
-        fe = e * de * de
-        east_before = east[l, j, pl.ds(r, n), :]
-        xb = x2[l, j - 1 + jnp.where(j == 0, 1, 0), at, :]
-        dw = x - prev_col(xb, x, n)
-        ew = prev_col(east_before, e, n)
-        sum_ = (fe + ew * dw * dw) + (s * ds_ * ds_ + s_up * dn * dn)
-        heats[l, j, pl.ds(r, n), :] = 0.05 * sum_ + (0.1 * g) * x * x
-
-    def sweep(fn, parts):
-        def zero(l):
-            flux[l] = jnp.zeros((ROWS, LANES), F32)
-        for l in range(2):
-            zero(l)
-
-        def body(j, carry):
-            for l in range(2):
-                for r, n in parts:
-                    fn(j, l, r, n)
-            return carry
-        lax.fori_loop(0, tiles, body, 0)
+        e, w, s, s_up, g = edges(l, j, r, n)
+        x, de, dw, ds_, dn = differences(x2, l, j, r, n)
+        total = (e * de * de + w * dw * dw) + (s * ds_ * ds_ + s_up * dn * dn)
+        heats[l, j, pl.ds(r, n), :] = 0.05 * total + (0.1 * g) * x * x
+
+    def sweep(fn, parts, unroll):
+        unroll = max(k for k in range(1, unroll + 1) if tiles % k == 0)
+
+        def body(k, carry):
+            for u in range(unroll):
+                for l in range(2):
+                    for r, n in parts:
+                        fn(k * unroll + u, l, r, n)
+            return carry
+        lax.fori_loop(0, tiles // unroll, body, 0)
 
     rim = ((0, 8), (ROWS - 8, 8))
 
@@ -371,15 +359,15 @@
         fetch(4, j).wait()
         return carry
     lax.fori_loop(0, tiles, wait_load, 0)
-    sweep(first, ((8, 24), (32, 24)))
+    sweep(first, ((8, 24), (32, 24)), 11)
     halo_recv(0, (res, x0))
-    sweep(first, rim)
+    sweep(first, rim, 11)
     halo_send(1, (x1,))
-    sweep(first, ((56, 32), (88, 32)))
+    sweep(first, ((56, 32), (88, 32)), 11)
     halo_recv(1, (x1,))
-    sweep(second, rim)
+    sweep(second, rim, 11)
     halo_send(2, (x2,))
-    sweep(second, ((8, 32), (40, 32), (72, 24), (96, 24)))
+    sweep(second, ((8, 32), (40, 32), (72, 24), (96, 24)), 11)
     halo_recv(2, (x2,))
 
     def drop_out(j):
@@ -549,7 +537,7 @@
     vm = pltpu.VMEM
     dma = pltpu.SemaphoreType.DMA
     field = vm((2, tiles, ROWS, LANES), F32)
-    padded = vm((2, tiles + 1, wide, LANES), F32)
+    padded = vm((2, tiles, wide, LANES), F32)
     column = vm((tiles, ROWS, LANES), F32)
     part = vm((half, ROWS, LANES), F32)
     return pl.pallas_call(
@@ -564,10 +552,9 @@
             field,
             padded, padded, padded, padded,
             field, field,
-            vm((2, tiles + 1, ROWS, LANES), F32),
+            field, field,
             vm((2, tiles, ROWS + PAD, LANES), F32),
-            vm((2, ROWS, LANES), F32),
-            vm((2, 8, LANES), F32),
+                vm((2, 8, LANES), F32),
             column, column, column, column,
             column, column, column, column,
             part, part, part, part,

time: 65.5 us -> 60.8 us (0.928)
  the two profiles are of different devices: /device:TPU:99 before, /device:TPU:32 now
where the time goes in v2:
time: 60.8 us; the launch traced here: 60.7 us
  Pallas kernels  54.8 us (90%)
  local copies, waits for them, and re-layouts  5.31 us (9%)
  between operations  0.65 us (1%)
    pallas_call x1, Pallas kernels, local(): pl.pallas_call(functools.partial(kernel, nt, nl, tiles), out_shape=(shape...  54.8 us
    unnamed x4, local copies, waits for them, and re-layouts  5.31 us

profile of v2, /device:TPU:32, one launch (start us, length us, event | category | flops | bytes accessed | tf_op | source)
XLA Modules:
  0.0 60.7 jit_solution(10775339815266103036)
XLA Ops:
  0.6 54.8 %shard_map.77 = (f32[2,128,2816]{2,1,0:T(8,128)}, f32[2,128,2816]{2,1,0:T(8,128)}) custom-call(f32[2,128,2816]{2,1,0:T(8,128)} %load_h.1, s32[2,128,2816]{2,1,0:T(8,128)} %cls_h.1, s32[2,128,2816]{2,1,0:T(8,128)} %via_h.1, f32[2,128,2816]{2,1,0:T(8,128)} %temp_h.1, f32[2,128,2816]{2,1,0:T(8,128)} %x0_h.1, f32[2,16]{1,0:T(2,128)} %table.1), custom_call_target="tpu_custom_call" | custom-call | flops 100000000 | bytes 20200000 | tf_op jit(solution)/shard_map/pallas_call | solution.py:543
  55.4 0.0 copy-start
  55.4 3.7 %copy.10 = f32[2,128,2816]{2,1,0:T(8,128)} copy(f32[2,128,2816]{2,1,0:T(8,128)} %get-tuple-element.4) | data formatting | bytes 5767168
  59.1 0.0 copy-done
  59.1 1.6 %copy.11 = f32[2,128,2816]{2,1,0:T(8,128)} copy(f32[2,128,2816]{2,1,0:T(8,128)S(1)} %copy-done) | data formatting | bytes 5767168
Async XLA Ops:
  55.4 3.7 %copy-start = (f32[2,128,2816]{2,1,0:T(8,128)S(1)}, f32[2,128,2816]{2,1,0:T(8,128)}, u32[]{:S(2)}) copy-start(f32[2,128,2816]{2,1,0:T(8,128)} %get-tuple-element.5) | copy-start | bytes 8650756

commit v3 on v2

--- a/solution.py
+++ b/solution.py
@@ -32,7 +32,7 @@
     load, cls, via, temp, x0, x1, x2, res, shunt, inv, east, west, south, tabs,
     ra, wa, rb, wb, pbuf, nbuf, pin, nin, mid_p, mid_n, t_own, t_far, t_in, t_out,
     h0s, h0r, h1s, h1r, h2s, h2r,
-    in_sem, out_sem, hs_sem, hr_sem,
+    temp_rim, cls_rim, x0_rim, rim_sem, in_sem, out_sem, hs_sem, hr_sem,
     p_ss, p_rs, n_ss, n_rs, mp_ss, mp_rs, mn_ss, mn_rs, mt_ss, mt_rs, t_ss, t_rs,
 ):
     d = lax.axis_index("layer")
@@ -57,12 +57,21 @@
         target = dst.at[:, j, pl.ds(PAD, ROWS), :] if k == 3 else dst.at[:, j]
         return pltpu.make_async_copy(src.at[:, :, cols(j)], target, in_sem.at[k, j])
 
-    for ks in ((0, 1), (2,), (3,), (4,)):
-        def start_in(i, carry, ks=ks):
-            for k in ks:
-                fetch(k, order(i)).start()
-            return carry
-        lax.fori_loop(0, tiles, start_in, 0)
+    def fetch_rim(k, side):
+        src, dst = ((temp_h, temp_rim), (cls_h, cls_rim), (x0_h, x0_rim))[k]
+        return pltpu.make_async_copy(
+            src.at[:, pl.ds(side * (ROWS - 8), 8), :], dst.at[side], rim_sem.at[k, side]
+        )
+
+    for k in range(3):
+        for side in range(2):
+            fetch_rim(k, side).start()
+
+    def start_in(i, carry):
+        fetch(0, order(i)).start()
+        fetch(1, order(i)).start()
+        return carry
+    lax.fori_loop(0, tiles, start_in, 0)
 
     barrier = pltpu.get_barrier_semaphore()
 
@@ -95,6 +104,22 @@
         h0r[1, 2:4] = jnp.zeros((2, 24, LANES), F32)
         h1r[1] = jnp.zeros((2, 24, LANES), F32)
         h2r[1] = jnp.zeros((2, 24, LANES), F32)
+
+    for k in range(3):
+        for side in range(2):
+            fetch_rim(k, side).wait()
+
+    def rim_pack(j, carry):
+        for side in range(2):
+            row = 7 * side
+            for l in range(2):
+                look = jnp.broadcast_to(tabs[l, 0:1, :], (8, LANES))
+                base = jnp.take_along_axis(look, cls_rim[side, l, :, cols(j)], axis=1)
+                own = base * (0.9025 + 0.0039 * temp_rim[side, l, :, cols(j)])
+                h0s[side, l, pl.ds(j, 1), :] = own[row : row + 1, :]
+                h0s[side, 2 + l, pl.ds(j, 1), :] = x0_rim[side, l, row : row + 1, cols(j)]
+        return carry
+    lax.fori_loop(0, tiles, rim_pack, 0)
 
     pl.semaphore_wait(
         barrier,
@@ -111,6 +136,12 @@
             device_id=(d, tile - 1 if up else tile + 1), device_id_type=MESH,
         )
 
+    def halo_start(stage):
+        for side, cond in ((0, north_ok), (1, south_ok)):
+            @pl.when(cond)
+            def _():
+                halo(stage, side).start()
+
     def halo_send(stage, fields):
         send = (h0s, h1s, h2s)[stage]
 
@@ -122,10 +153,7 @@
             return carry
 
         lax.fori_loop(0, tiles, pack, 0)
-        for side, cond in ((0, north_ok), (1, south_ok)):
-            @pl.when(cond)
-            def _():
-                halo(stage, side).start()
+        halo_start(stage)
 
     def halo_recv(stage, fields):
         recv = (h0r, h1r, h2r)[stage]
@@ -148,6 +176,8 @@
             @pl.when(cond)
             def _():
                 halo(stage, side).wait_send()
+
+    halo_start(0)
 
     def toward(i):
         return (jnp.where(low, d + 1, d - 1), tile)
@@ -215,17 +245,23 @@
                 db = w_b * db
             pbuf[i, rows, :] = db
 
+    def start_rest(i):
+        for k in (2, 3, 4):
+            fetch(k, order(i)).start()
+
     def outer_matrix(role):
         def body(i, carry):
             fetch(0, order(i)).wait()
             fetch(1, order(i)).wait()
             matrix(role, i)
             p_in(i).start()
+            start_rest(i)
             return carry
         lax.fori_loop(0, tiles, body, 0)
 
     def inner_matrix(role):
         def body(i, carry):
+            start_rest(i)
             fetch(0, order(i)).wait()
             fetch(1, order(i)).wait()
             p_in(i).wait_recv()
@@ -265,7 +301,6 @@
         return carry
 
     lax.fori_loop(0, tiles, resist, 0)
-    halo_send(0, (res, x0))
 
     def lane_of(n):
         return lax.broadcasted_iota(jnp.int32, (n, LANES), 1)
@@ -354,21 +389,23 @@
         lax.fori_loop(0, tiles // unroll, body, 0)
 
     rim = ((0, 8), (ROWS - 8, 8))
+    middle = ((8, 32), (40, 32), (72, 24), (96, 24))
 
     def wait_load(j, carry):
         fetch(4, j).wait()
         return carry
     lax.fori_loop(0, tiles, wait_load, 0)
-    sweep(first, ((8, 24), (32, 24)), 11)
     halo_recv(0, (res, x0))
     sweep(first, rim, 11)
     halo_send(1, (x1,))
-    sweep(first, ((56, 32), (88, 32)), 11)
+    sweep(first, middle, 11)
     halo_recv(1, (x1,))
     sweep(second, rim, 11)
     halo_send(2, (x2,))
-    sweep(second, ((8, 32), (40, 32), (72, 24), (96, 24)), 11)
+    sweep(second, middle, 11)
+    sweep(heat, middle, 11)
     halo_recv(2, (x2,))
+    sweep(heat, rim, 11)
 
     def drop_out(j):
         return pltpu.make_async_copy(
@@ -412,9 +449,6 @@
     def heat_step(i, carry):
         j = order(i)
         drop_out(j).start()
-        for l in range(2):
-            for r in range(0, ROWS, 32):
-                heat(j, l, r, 32)
 
         @pl.when(d == 0)
         def _():
@@ -542,9 +576,9 @@
     part = vm((half, ROWS, LANES), F32)
     return pl.pallas_call(
         functools.partial(kernel, nt, nl, tiles),
-        out_shape=(shape, shape),
+        out_shape=(pltpu.VMEM(load_current.shape, F32), pltpu.VMEM(load_current.shape, F32)),
         in_specs=[pl.BlockSpec(memory_space=pl.ANY)] * 5 + [pl.BlockSpec(memory_space=pltpu.VMEM)],
-        out_specs=[pl.BlockSpec(memory_space=pl.ANY)] * 2,
+        out_specs=[pl.BlockSpec(memory_space=pltpu.VMEM)] * 2,
         scratch_shapes=[
             field,
             vm((2, tiles, ROWS, LANES), jnp.int32),
@@ -562,13 +596,14 @@
             vm((2, 4, 24, LANES), F32), vm((2, 4, 24, LANES), F32),
             vm((2, 2, 24, LANES), F32), vm((2, 2, 24, LANES), F32),
             vm((2, 2, 24, LANES), F32), vm((2, 2, 24, LANES), F32),
-            dma((5, tiles)), dma((2, tiles)), dma((3, 2)), dma((3, 2)),
+            vm((2, 2, 8, tiles * LANES), F32), vm((2, 2, 8, tiles * LANES), jnp.int32),
+            vm((2, 2, 8, tiles * LANES), F32), dma((3, 2)), dma((5, tiles)), dma((2, tiles)), dma((3, 2)), dma((3, 2)),
             dma((tiles,)), dma((tiles,)), dma((tiles,)), dma((tiles,)),
             dma((half,)), dma((half,)), dma((half,)), dma((half,)),
             dma((half,)), dma((half,)), dma((tiles,)), dma((tiles,)),
         ],
         compiler_params=pltpu.CompilerParams(
-            collective_id=0, has_side_effects=True, vmem_limit_bytes=63000000
+            collective_id=0, has_side_effects=True, vmem_limit_bytes=59000000
         ),
         cost_estimate=pl.CostEstimate(flops=100000000, bytes_accessed=20200000, transcendentals=5000000),
     )(load_current, metal_class, via_mask, temp_prior, drop_prior, class_conductance)

time: 60.8 us -> 52.3 us (0.86)
  the two profiles are of different devices: /device:TPU:32 before, /device:TPU:99 now
where the time goes in v3:
time: 52.3 us; the launch traced here: 51.6 us
  Pallas kernels  47.8 us (91%)
  local copies, waits for them, and re-layouts  3.16 us (6%)
  between operations  0.64 us (1%)
    pallas_call x1, Pallas kernels, local(): pl.pallas_call(functools.partial(kernel, nt, nl, tiles), out_shape=(pltpu...  47.8 us
    unnamed x2, local copies, waits for them, and re-layouts  3.16 us

profile of v3, /device:TPU:99, one launch (start us, length us, event | category | flops | bytes accessed | tf_op | source)
XLA Modules:
  0.0 51.6 jit_solution(17133787134754296018)
XLA Ops:
  0.6 47.8 %shard_map.77 = (f32[2,128,2816]{2,1,0:T(8,128)S(1)}, f32[2,128,2816]{2,1,0:T(8,128)S(1)}) custom-call(f32[2,128,2816]{2,1,0:T(8,128)} %load_h.1, s32[2,128,2816]{2,1,0:T(8,128)} %cls_h.1, s32[2,128,2816]{2,1,0:T(8,128)} %via_h.1, f32[2,128,2816]{2,1,0:T(8,128)} %temp_h.1, f32[2,128,2816]{2,1,0:T(8,128)} %x0_h.1, f32[2,16]{1,0:T(2,128)} %table.1), custom_call_target="tpu_custom_call" | custom-call | flops 100000000 | bytes 20200000 | tf_op jit(solution)/shard_map/pallas_call | solution.py:577
  48.5 1.6 %copy.10 = f32[2,128,2816]{2,1,0:T(8,128)} copy(f32[2,128,2816]{2,1,0:T(8,128)S(1)} %get-tuple-element.2) | data formatting | bytes 5767168
  50.0 1.6 %copy.11 = f32[2,128,2816]{2,1,0:T(8,128)} copy(f32[2,128,2816]{2,1,0:T(8,128)S(1)} %get-tuple-element.3) | data formatting | bytes 5767168

commit v4 on v3

--- a/solution.py
+++ b/solution.py
@@ -11,6 +11,7 @@
 F32 = jnp.float32
 ROWS = 128
 LANES = 128
+CHAINS = 64
 PAD = 8
 HALF_WIDTH = 0.9
 RHO_ONE = 0.9
@@ -38,14 +39,14 @@
     d = lax.axis_index("layer")
     tile = lax.axis_index("tile")
     half = tiles // 2
+    early = half // 3 + 1
     low = d < nl // 2
     outer = jnp.logical_or(d == 0, d == nl - 1)
     inner = jnp.logical_not(outer)
     heats = temp
 
     def order(i):
-        j = i + jnp.where(low, half, 0)
-        return jnp.where(j >= tiles, j - tiles, j)
+        return jnp.where(low, tiles - 1 - i, i)
 
     def cols(j):
         return pl.ds(pl.multiple_of(j * LANES, LANES), LANES)
@@ -109,15 +110,16 @@
         for side in range(2):
             fetch_rim(k, side).wait()
 
-    def rim_pack(j, carry):
+    def rim_pack(i, carry):
+        j = order(i)
         for side in range(2):
             row = 7 * side
             for l in range(2):
                 look = jnp.broadcast_to(tabs[l, 0:1, :], (8, LANES))
                 base = jnp.take_along_axis(look, cls_rim[side, l, :, cols(j)], axis=1)
                 own = base * (0.9025 + 0.0039 * temp_rim[side, l, :, cols(j)])
-                h0s[side, l, pl.ds(j, 1), :] = own[row : row + 1, :]
-                h0s[side, 2 + l, pl.ds(j, 1), :] = x0_rim[side, l, row : row + 1, cols(j)]
+                h0s[side, l, pl.ds(i, 1), :] = own[row : row + 1, :]
+                h0s[side, 2 + l, pl.ds(i, 1), :] = x0_rim[side, l, row : row + 1, cols(j)]
         return carry
     lax.fori_loop(0, tiles, rim_pack, 0)
 
@@ -142,34 +144,36 @@
             def _():
                 halo(stage, side).start()
 
-    def halo_send(stage, fields):
+    def halo_send(stage, fields, lo, hi):
         send = (h0s, h1s, h2s)[stage]
 
-        def pack(j, carry):
+        def pack(i, carry):
+            j = order(i)
             for f, ref in enumerate(fields):
                 for l in range(2):
-                    send[0, 2 * f + l, pl.ds(j, 1), :] = ref[l, j, PAD : PAD + 1, :]
-                    send[1, 2 * f + l, pl.ds(j, 1), :] = ref[l, j, PAD + ROWS - 1 : PAD + ROWS, :]
-            return carry
-
-        lax.fori_loop(0, tiles, pack, 0)
+                    send[0, 2 * f + l, pl.ds(i - lo, 1), :] = ref[l, j, PAD : PAD + 1, :]
+                    send[1, 2 * f + l, pl.ds(i - lo, 1), :] = ref[l, j, PAD + ROWS - 1 : PAD + ROWS, :]
+            return carry
+
+        lax.fori_loop(lo, hi, pack, 0)
         halo_start(stage)
 
-    def halo_recv(stage, fields):
+    def halo_recv(stage, fields, lo, hi):
         recv = (h0r, h1r, h2r)[stage]
         for side, cond in ((0, north_ok), (1, south_ok)):
             @pl.when(cond)
             def _():
                 halo(stage, 1 - side, True).wait_recv()
 
-        def unpack(j, carry):
+        def unpack(i, carry):
+            j = order(i)
             for f, ref in enumerate(fields):
                 for l in range(2):
-                    ref[l, j, PAD - 1 : PAD, :] = recv[0, 2 * f + l, pl.ds(j, 1), :]
-                    ref[l, j, PAD + ROWS : PAD + ROWS + 1, :] = recv[1, 2 * f + l, pl.ds(j, 1), :]
-            return carry
-
-        lax.fori_loop(0, tiles, unpack, 0)
+                    ref[l, j, PAD - 1 : PAD, :] = recv[0, 2 * f + l, pl.ds(i - lo, 1), :]
+                    ref[l, j, PAD + ROWS : PAD + ROWS + 1, :] = recv[1, 2 * f + l, pl.ds(i - lo, 1), :]
+            return carry
+
+        lax.fori_loop(lo, hi, unpack, 0)
 
     def halo_done(stage):
         for side, cond in ((0, north_ok), (1, south_ok)):
@@ -185,9 +189,10 @@
     def away(i):
         return (jnp.where(low, jnp.where(d == 0, d + 1, d - 1), jnp.where(d == nl - 1, d - 1, d + 1)), tile)
 
-    def remote(src, dst, ss, rs, j, where):
+    def remote(src, dst, ss, rs, j, where, to=None):
+        k = j if to is None else to
         return pltpu.make_async_remote_copy(
-            src_ref=src.at[j], dst_ref=dst.at[j], send_sem=ss.at[j], recv_sem=rs.at[j],
+            src_ref=src.at[j], dst_ref=dst.at[k], send_sem=ss.at[j], recv_sem=rs.at[k],
             device_id=where, device_id_type=MESH,
         )
 
@@ -198,13 +203,13 @@
         return remote(nbuf, nin, n_ss, n_rs, i, toward(i))
 
     def p_mid(i):
-        return remote(pbuf, mid_p, mp_ss, mp_rs, i, toward(i))
+        return remote(pbuf, mid_p, mp_ss, mp_rs, i, toward(i), half - 1 - i)
 
     def n_mid(i):
-        return remote(nbuf, mid_n, mn_ss, mn_rs, i, toward(i))
+        return remote(nbuf, mid_n, mn_ss, mn_rs, i, toward(i), half - 1 - i)
 
     def t_mid(i):
-        return remote(t_own, t_far, mt_ss, mt_rs, i, toward(i))
+        return remote(t_own, t_far, mt_ss, mt_rs, i, toward(i), half - 1 - i)
 
     def t_back(i):
         return remote(t_out, t_in, t_ss, t_rs, i, away(i))
@@ -267,7 +272,7 @@
             p_in(i).wait_recv()
             matrix(role, i)
 
-            @pl.when(i < half)
+            @pl.when(i < early)
             def _():
                 p_mid(i).start()
             return carry
@@ -377,35 +382,27 @@
         total = (e * de * de + w * dw * dw) + (s * ds_ * ds_ + s_up * dn * dn)
         heats[l, j, pl.ds(r, n), :] = 0.05 * total + (0.1 * g) * x * x
 
-    def sweep(fn, parts, unroll):
-        unroll = max(k for k in range(1, unroll + 1) if tiles % k == 0)
-
-        def body(k, carry):
-            for u in range(unroll):
+    def sweep(fn, parts, lo, hi):
+        unroll = max(1, min(hi - lo, CHAINS // (2 * sum(n for _, n in parts) // 8)))
+        full = (hi - lo) // unroll
+
+        def step(start, count):
+            for u in range(count):
+                j = order(start + u)
                 for l in range(2):
                     for r, n in parts:
-                        fn(k * unroll + u, l, r, n)
-            return carry
-        lax.fori_loop(0, tiles // unroll, body, 0)
+                        fn(j, l, r, n)
+
+        def body(k, carry):
+            step(lo + k * unroll, unroll)
+            return carry
+        lax.fori_loop(0, full, body, 0)
+        if lo + full * unroll < hi:
+            step(lo + full * unroll, hi - lo - full * unroll)
 
     rim = ((0, 8), (ROWS - 8, 8))
+    core = ((16, 32), (48, 32), (80, 32))
     middle = ((8, 32), (40, 32), (72, 24), (96, 24))
-
-    def wait_load(j, carry):
-        fetch(4, j).wait()
-        return carry
-    lax.fori_loop(0, tiles, wait_load, 0)
-    halo_recv(0, (res, x0))
-    sweep(first, rim, 11)
-    halo_send(1, (x1,))
-    sweep(first, middle, 11)
-    halo_recv(1, (x1,))
-    sweep(second, rim, 11)
-    halo_send(2, (x2,))
-    sweep(second, middle, 11)
-    sweep(heat, middle, 11)
-    halo_recv(2, (x2,))
-    sweep(heat, rim, 11)
 
     def drop_out(j):
         return pltpu.make_async_copy(
@@ -431,43 +428,67 @@
             heats[b, j, rows, :] = nb
             nbuf[i, rows, :] = wb[i, rows, :] * nb if role < 2 else nb
 
-    def inner_right(i):
-        n_in(i).wait_recv()
-
-        @pl.when(d == 1)
-        def _():
-            right_side(1, i)
-
-        @pl.when(d == 2)
-        def _():
-            right_side(2, i)
-
-        @pl.when(i < half)
-        def _():
-            n_mid(i).start()
-
-    def heat_step(i, carry):
-        j = order(i)
+    def right_outer(lo, hi):
+        for role, where in ((0, 0), (3, nl - 1)):
+            @pl.when(d == where)
+            def _(role=role):
+                def body(i, carry):
+                    right_side(role, i)
+                    n_in(i).start()
+                    return carry
+                lax.fori_loop(lo, hi, body, 0)
+
+    def right_inner(lo, hi):
+        for role in (1, 2):
+            @pl.when(d == role)
+            def _(role=role):
+                def body(i, carry):
+                    n_in(i).wait_recv()
+                    right_side(role, i)
+                    if hi <= half:
+                        n_mid(i).start()
+                    return carry
+                lax.fori_loop(lo, hi, body, 0)
+
+    def wait_load(j, carry):
+        fetch(4, j).wait()
+        return carry
+
+    def start_drop(j, carry):
         drop_out(j).start()
-
-        @pl.when(d == 0)
-        def _():
-            right_side(0, i)
-
-        @pl.when(d == nl - 1)
-        def _():
-            right_side(3, i)
-
-        @pl.when(outer)
-        def _():
-            n_in(i).start()
-
-        @pl.when(jnp.logical_and(inner, i >= 2))
-        def _():
-            inner_right(i - 2)
         return carry
 
-    lax.fori_loop(0, tiles, heat_step, 0)
+    two = min(half + 3, tiles)
+    one = min(half + 1, tiles)
+    lax.fori_loop(0, tiles, wait_load, 0)
+    halo_recv(0, (res, x0), 0, tiles)
+    sweep(first, ((0, 16), (ROWS - 16, 16)), 0, tiles)
+    halo_send(1, (x1,), 0, tiles)
+
+    @pl.when(inner)
+    def _():
+        def send_rest(i, carry):
+            p_mid(i).start()
+            return carry
+        lax.fori_loop(early, half, send_rest, 0)
+
+    sweep(first, core, 0, two)
+    halo_recv(1, (x1,), 0, tiles)
+    sweep(second, rim, 0, tiles)
+    halo_send(2, (x2,), 0, tiles)
+    sweep(second, middle, 0, one)
+    sweep(heat, middle, 0, half)
+    halo_recv(2, (x2,), 0, tiles)
+    sweep(heat, rim, 0, half)
+    right_outer(0, half)
+    sweep(first, core, two, (two + tiles) // 2)
+    right_inner(0, half)
+    sweep(first, core, (two + tiles) // 2, tiles)
+    sweep(second, middle, one, tiles)
+    sweep(heat, rim + middle, half, tiles)
+    lax.fori_loop(0, tiles, start_drop, 0)
+    right_outer(half, tiles)
+    right_inner(half, tiles)
 
     def back(role, i):
         j = order(i)
@@ -497,13 +518,11 @@
 
     @pl.when(inner)
     def _():
-        inner_right(tiles - 2)
-        inner_right(tiles - 1)
-
-        def own(k, carry):
+        def own(kk, carry):
+            k = half - 1 - kk
             i = half + k
-            p_mid(k).wait_recv()
-            n_mid(k).wait_recv()
+            p_mid(kk).wait_recv()
+            n_mid(kk).wait_recv()
             for r in range(0, ROWS, 32):
                 rows = pl.ds(r, 32)
                 t4 = (nbuf[i, rows, :] + mid_n[k, rows, :]) * rcp(pbuf[i, rows, :] + mid_p[k, rows, :])
@@ -515,7 +534,7 @@
         lax.fori_loop(0, half, own, 0)
 
         def far(k, carry):
-            t_mid(k).wait_recv()
+            t_mid(half - 1 - k).wait_recv()
             t_in[k] = t_far[k]
             inner_back(k)
             return carry
@@ -524,8 +543,7 @@
     @pl.when(outer)
     def _():
         def last(k, carry):
-            i = k + half
-            i = jnp.where(i >= tiles, i - tiles, i)
+            i = jnp.where(k < half, tiles - 1 - k, k - half)
             t_back(i).wait_recv()
 
             @pl.when(d == 0)

time: 52.3 us -> 51.9 us (level); the launches traced: 51.6 us -> 51.8 us
  no operation moved by 1% of the time
where the time goes in v4:
time: 51.9 us; the launch traced here: 51.8 us
  Pallas kernels  48 us (92%)
  local copies, waits for them, and re-layouts  3.16 us (6%)
  between operations  0.64 us (1%)
    pallas_call x1, Pallas kernels, local(): pl.pallas_call(functools.partial(kernel, nt, nl, tiles), out_shape=(pltpu...  48 us
    unnamed x2, local copies, waits for them, and re-layouts  3.16 us

profile of v4, /device:TPU:99, one launch (start us, length us, event | category | flops | bytes accessed | tf_op | source)
XLA Modules:
  0.0 51.8 jit_solution(12084576817747643875)
XLA Ops:
  0.6 48.0 %shard_map.77 = (f32[2,128,2816]{2,1,0:T(8,128)S(1)}, f32[2,128,2816]{2,1,0:T(8,128)S(1)}) custom-call(f32[2,128,2816]{2,1,0:T(8,128)} %load_h.1, s32[2,128,2816]{2,1,0:T(8,128)} %cls_h.1, s32[2,128,2816]{2,1,0:T(8,128)} %via_h.1, f32[2,128,2816]{2,1,0:T(8,128)} %temp_h.1, f32[2,128,2816]{2,1,0:T(8,128)} %x0_h.1, f32[2,16]{1,0:T(2,128)} %table.1), custom_call_target="tpu_custom_call" | custom-call | flops 100000000 | bytes 20200000 | tf_op jit(solution)/shard_map/pallas_call | solution.py:595
  48.7 1.6 %copy.10 = f32[2,128,2816]{2,1,0:T(8,128)} copy(f32[2,128,2816]{2,1,0:T(8,128)S(1)} %get-tuple-element.2) | data formatting | bytes 5767168
  50.2 1.6 %copy.11 = f32[2,128,2816]{2,1,0:T(8,128)} copy(f32[2,128,2816]{2,1,0:T(8,128)S(1)} %get-tuple-element.3) | data formatting | bytes 5767168
